TPU v7x, 32 devices: a whole 2x2x4 slice. The times are simulated.
32 devices in a mesh: dp: 4 (over y, core), fsdp: 4 (over z), seq: 2 (over x).
Axes of the slice: x: 2, y: 2, z: 4, core: 2. Of those that a mesh axis runs over, the one named last changes fastest.
Arguments:
- queries: bfloat16 [16, 256, 2048], P(('dp', 'fsdp'), 'seq'), may hold values from -30 to 30
- key_rows: bfloat16 [16, 256, 2048], P(('dp', 'fsdp'), 'seq'), may hold values from -12 to 12
- value_rows: bfloat16 [16, 256, 2048], P(('dp', 'fsdp'), 'seq'), may hold values from -6 to 6
- cotangent: bfloat16 [16, 256, 2048], P(('dp', 'fsdp'), 'seq'), may hold values from -6 to 6
- out_weight: bfloat16 [2048, 2048], P('fsdp'), may hold values from -0.125 to 0.125
Outputs:
- query_grad: bfloat16 [16, 256, 2048], P(('dp', 'fsdp'), 'seq')
- key_grad: bfloat16 [16, 256, 2048], P(('dp', 'fsdp'), 'seq')
- value_grad: bfloat16 [16, 256, 2048], P(('dp', 'fsdp'), 'seq')
- weight_grad: float32 [2048, 2048], P('fsdp')
All inputs are finite; a program needn't handle non-finite values.
Results may differ from a plain program's by a relative error of at most 0.014.
Values may be sent and summed in bfloat16 or wider, within the bound.
A program may use at most 128 MiB of HBM per device.

v0:
```python
import jax
import jax.numpy as jnp
from jax import lax
from jax.sharding import PartitionSpec as P

DH = 128


def head_backward(query_head, key_head, value_head, grad_head, block_rows):
    length = key_head.shape[0]
    score_scale = DH ** (-0.5)
    blocks = length // block_rows

    def visit(carry, block):
        key_acc, value_acc = carry
        begin = block * block_rows
        query_block = lax.dynamic_slice_in_dim(query_head, begin, block_rows, 0)
        grad_block = lax.dynamic_slice_in_dim(grad_head, begin, block_rows, 0)
        scores = (
            jnp.einsum("qd,kd->qk", query_block, key_head, preferred_element_type=jnp.float32)
            * score_scale
        )
        highest = jnp.max(scores, axis=1, keepdims=True)
        expanded = jnp.exp(scores - highest)
        weights = expanded / jnp.sum(expanded, axis=1, keepdims=True)
        weights_half = weights.astype(jnp.bfloat16)
        attended = jnp.einsum(
            "qk,kd->qd", weights_half, value_head, preferred_element_type=jnp.float32
        ).astype(jnp.bfloat16)
        grad_weights = jnp.einsum(
            "qd,kd->qk", grad_block, value_head, preferred_element_type=jnp.float32
        )
        row_delta = jnp.sum(weights * grad_weights, axis=1, keepdims=True)
        grad_scores = (weights * (grad_weights - row_delta)).astype(jnp.bfloat16)
        query_grad = (
            jnp.einsum("qk,kd->qd", grad_scores, key_head, preferred_element_type=jnp.float32)
            * score_scale
        ).astype(jnp.bfloat16)
        key_acc = key_acc + jnp.einsum(
            "qk,qd->kd", grad_scores, query_block, preferred_element_type=jnp.float32
        )
        value_acc = value_acc + jnp.einsum(
            "qk,qd->kd", weights_half, grad_block, preferred_element_type=jnp.float32
        )
        return ((key_acc, value_acc), (attended, query_grad))

    empty = jnp.zeros(key_head.shape, jnp.float32)
    finals, stacked = lax.scan(visit, (empty, empty), jnp.arange(blocks))
    attended = stacked[0].reshape(length, DH)
    query_grad = stacked[1].reshape(length, DH)
    key_grad = (finals[0] * score_scale).astype(jnp.bfloat16)
    value_grad = finals[1].astype(jnp.bfloat16)
    return (attended, query_grad, key_grad, value_grad)


def attend_heads(query_heads, key_heads, value_heads, grad_heads):
    length = query_heads.shape[1]
    per_device = query_heads.shape[2] // DH
    block_rows = min(512, length)
    gathered = [[], [], [], []]
    for head_index in range(per_device):
        lower = head_index * DH
        upper = lower + DH
        results = head_backward(
            query_heads[0, :, lower:upper],
            key_heads[0, :, lower:upper],
            value_heads[0, :, lower:upper],
            grad_heads[0, :, lower:upper],
            block_rows,
        )
        for position, result in enumerate(results):
            gathered[position].append(result)
    return tuple((jnp.concatenate(group, axis=1)[None] for group in gathered))


def body(queries, key_rows, value_rows, cotangent, out_weight):
    samples = lax.axis_size("dp") * lax.axis_size("fsdp")
    grad_out = jnp.einsum(
        "btd,rd->btr",
        cotangent,
        lax.all_gather(out_weight, "fsdp", axis=0, tiled=True),
        preferred_element_type=jnp.float32,
    ).astype(jnp.bfloat16)
    query_heads, key_heads, value_heads, grad_heads = (
        lax.all_to_all(queries, "seq", split_axis=2, concat_axis=1, tiled=True),
        lax.all_to_all(key_rows, "seq", split_axis=2, concat_axis=1, tiled=True),
        lax.all_to_all(value_rows, "seq", split_axis=2, concat_axis=1, tiled=True),
        lax.all_to_all(grad_out, "seq", split_axis=2, concat_axis=1, tiled=True),
    )
    head_results = attend_heads(query_heads, key_heads, value_heads, grad_heads)
    attended, query_grad, key_grad, value_grad = (
        lax.all_to_all(head_results[0], "seq", split_axis=1, concat_axis=2, tiled=True),
        lax.all_to_all(head_results[1], "seq", split_axis=1, concat_axis=2, tiled=True),
        lax.all_to_all(head_results[2], "seq", split_axis=1, concat_axis=2, tiled=True),
        lax.all_to_all(head_results[3], "seq", split_axis=1, concat_axis=2, tiled=True),
    )
    shares = lax.psum_scatter(
        jnp.einsum("btr,btd->rd", attended, cotangent, preferred_element_type=jnp.float32),
        ("fsdp", "seq"),
        scatter_dimension=0,
        tiled=True,
    )
    shares = lax.psum(shares.astype(jnp.bfloat16), "dp").astype(jnp.float32)
    total = lax.all_gather(shares.astype(jnp.bfloat16), "seq", axis=0, tiled=True).astype(
        shares.dtype
    )
    return (query_grad, key_grad, value_grad, total / samples)


def solution(mesh):
    return jax.shard_map(
        body,
        mesh=mesh,
        in_specs=(
            P(("dp", "fsdp"), "seq", None),
            P(("dp", "fsdp"), "seq", None),
            P(("dp", "fsdp"), "seq", None),
            P(("dp", "fsdp"), "seq", None),
            P("fsdp", None),
        ),
        out_specs=(
            P(("dp", "fsdp"), "seq", None),
            P(("dp", "fsdp"), "seq", None),
            P(("dp", "fsdp"), "seq", None),
            P("fsdp", None),
        ),
        check_vma=False,
    )
```

profile of v0, /device:TPU:0, one launch (start us, length us, event | category | flops | bytes accessed | tf_op | source)
XLA Modules:
  0.0 528.8 jit_solution(7082781794581919626)
XLA Ops:
  8.8 2.4 copy.55
  11.7 11.6 %reduce.1 = bf16[2048,128]{1,0:T(8,128)(2,1)S(1)} reduce(bf16[2048,1,128]{2,1,0:T(2,128)(2,1)S(1)} %bitcast.293, bf16[]{:T(256)} %broadcast.90), dimensions={1}, to_apply=%bitcast.175.reduce_sub_computation | reduce | bytes 1048578
  23.3 0.9 reshape.80
  24.2 4.2 all-to-all-start
  29.2 11.6 %reduce = bf16[2048,128]{1,0:T(8,128)(2,1)S(1)} reduce(bf16[2048,1,128]{2,1,0:T(2,128)(2,1)S(1)} %bitcast.299, bf16[]{:T(256)} %broadcast.90), dimensions={1}, to_apply=%bitcast.177.reduce_sub_computation | reduce | bytes 1048578
  40.7 0.9 reshape.82
  41.6 3.7 all-to-all-start.1
  46.1 11.6 %reduce.2 = bf16[2048,128]{1,0:T(8,128)(2,1)S(1)} reduce(bf16[2048,1,128]{2,1,0:T(2,128)(2,1)S(1)} %bitcast.300, bf16[]{:T(256)} %broadcast.90), dimensions={1}, to_apply=%bitcast.173.reduce_sub_computation | reduce | bytes 1048578
  57.6 0.9 reshape.78
  58.5 3.5 all-to-all-start.3
  62.6 1.0 copy.56
  64.2 1.0 copy.58
  65.2 5.5 %all-to-all-done.3 = bf16[2,2,65536]{2,1,0:T(2,128)(2,1)S(1)} async-done(((bf16[2,2,65536]{2,1,0:T(2,128)(2,1)}), bf16[2,2,65536]{2,1,0:T(2,128)(2,1)S(1)}, u32[]{:S(2)}, u32[]{:S(2)}) %all-to-all-start.3) | async-done | bytes 524320 | tf_op jit(solution)/shard_map/all_to_all | solution.py:87
  71.5 1.3 fusion.115
  72.9 1.1 fusion.114
  74.0 1.1 fusion.113
  75.2 1.1 fusion.112
  76.4 1.1 fusion.111
  77.6 1.1 fusion.110
  78.7 1.1 fusion.109
  79.9 1.1 fusion.108
  83.7 2.5 copy.69
  86.2 4.5 reduce.7
  90.7 1.4 reshape.90
  92.1 11.1 %all_to_all.141 = bf16[2,2,65536]{2,1,0:T(2,128)(2,1)} all-to-all(bf16[2,2,65536]{2,1,0:T(2,128)(2,1)S(1)} %reshape.90), channel_id=1, replica_groups=mesh['dp'=4,'fsdp'=4,'seq'=2] {'seq'}, dimensions={0} | all-to-all | bytes 1048576 | tf_op jit(solution)/shard_map/all_to_all | solution.py:92
  103.2 1.4 reshape.91
  104.6 1.0 copy.81
  105.6 1.3 copy.70
  106.9 8.0 %fusion.49 = f32[2048,2048]{1,0:T(8,128)} fusion(bf16[128,2048]{0,1:T(8,128)(2,1)S(1)} %bitcast.301, bf16[1,128,2048]{2,1,0:T(8,128)(2,1)S(1)} %copy-done), kind=kOutput, calls=%fused_computation.91 | convolution fusion | flops 1073741824 | bytes 17825792 | tf_op jit(solution)/shard_map/btr,btd->rd/dot_general | solution.py:98
  115.0 48.1 %all-gather.3.cloned.1.call-done = bf16[2048,2048]{1,0:T(8,128)(2,1)} async-done(((bf16[512,2048]{1,0:T(8,128)(2,1)}), bf16[2048,2048]{1,0:T(8,128)(2,1)}) %all-gather.3.cloned.1.call-update) | async-done | bytes 8388624 | tf_op jit(solution)/shard_map/all_gather | solution.py:81
  163.1 7.1 %fusion = bf16[1,128,2048]{2,1,0:T(8,128)(2,1)} fusion(bf16[2048,2048]{1,0:T(8,128)(2,1)} %all-gather.3.cloned.1.call-done, bf16[1,128,2048]{2,1,0:T(8,128)(2,1)S(1)} %copy-done), kind=kOutput, calls=%fused_computation.2 | convolution fusion | flops 1074003968 | bytes 9437184 | tf_op jit(solution)/shard_map/btd,rd->btr/dot_general | solution.py:78
  170.1 2.3 copy.59
  172.5 12.4 %reduce.3 = bf16[2048,128]{1,0:T(8,128)(2,1)} reduce(bf16[2048,1,128]{2,1,0:T(2,128)(2,1)S(1)} %bitcast.296, bf16[]{:T(256)} %broadcast.90), dimensions={1}, to_apply=%bitcast.171.reduce_sub_computation | reduce | bytes 1048578
  184.9 1.1 reshape.76
  186.0 17.7 %all_to_all.142 = bf16[2,2,65536]{2,1,0:T(2,128)(2,1)} all-to-all(bf16[2,2,65536]{2,1,0:T(2,128)(2,1)S(1)} %reshape.76), channel_id=1, replica_groups=mesh['dp'=4,'fsdp'=4,'seq'=2] {'seq'}, dimensions={0} | all-to-all | bytes 1048576 | tf_op jit(solution)/shard_map/all_to_all | solution.py:88
  203.7 1.4 reshape.77
  206.0 1.2 copy.60
  209.9 2.5 copy.67
  212.4 4.5 reduce.6
  216.9 2.1 reshape.88
  219.1 3.5 all-to-all-start.6
  222.6 1.3 multiply_reduce_fusion.7
  224.0 1.0 multiply_convert_fusion.7
  225.5 1.1 multiply_reduce_fusion.6
  230.4 0.9 multiply_reduce_fusion.1
  231.6 201.0 %reduce-scatter.2.cloned.1.call-done = f32[256,2048]{1,0:T(8,128)} async-done(((f32[2048,2048]{1,0:T(8,128)}), f32[256,2048]{1,0:T(8,128)}) %reduce-scatter.2.cloned.1.call-update) | async-done | bytes 2097168 | tf_op jit(solution)/shard_map/reduce_scatter | solution.py:97
  432.5 2.7 convert_element_type.240
  435.7 1.0 multiply_convert_fusion.1
  436.8 34.4 %all-reduce.2.cloned.1.call-done = bf16[256,2048]{1,0:T(8,128)(2,1)} async-done(((bf16[256,2048]{1,0:T(8,128)(2,1)}), bf16[256,2048]{1,0:T(8,128)(2,1)}) %all-reduce.2.cloned.1.call-update) | async-done | bytes 1048592 | tf_op jit(solution)/shard_map/psum | solution.py:103
  471.7 1.1 multiply_reduce_fusion
  473.1 1.0 copy.63
  474.1 3.7 reduce.4
  477.8 1.1 reshape.84
  479.8 3.5 all-to-all-start.4
  485.0 2.5 copy.65
  487.5 3.7 reduce.5
  491.3 1.1 reshape.86
  492.4 5.0 all-to-all-done.4
  497.3 3.5 all-to-all-start.5
  501.8 1.0 copy.73
  503.7 1.0 copy.71
  504.8 9.8 %all-to-all-done.5 = bf16[2,2,65536]{2,1,0:T(2,128)(2,1)S(1)} async-done(((bf16[2,2,65536]{2,1,0:T(2,128)(2,1)}), bf16[2,2,65536]{2,1,0:T(2,128)(2,1)S(1)}, u32[]{:S(2)}, u32[]{:S(2)}) %all-to-all-start.5) | async-done | bytes 524320 | tf_op jit(solution)/shard_map/all_to_all | solution.py:94
  515.5 1.0 copy.72
  516.8 4.2 convert_multiply_fusion
  (116 shorter events, 22.7 us)
Async XLA Ops:
  8.0 98.9 %copy-start = (bf16[1,128,2048]{2,1,0:T(8,128)(2,1)S(1)}, bf16[1,128,2048]{2,1,0:T(8,128)(2,1)}, u32[]{:S(2)}) copy-start(bf16[1,128,2048]{2,1,0:T(8,128)(2,1)} %param.8) | copy-start | bytes 1572868
  8.0 20.4 %copy-start.6 = (bf16[1,128,2048]{2,1,0:T(8,128)(2,1)S(1)}, bf16[1,128,2048]{2,1,0:T(8,128)(2,1)}, u32[]{:S(2)}) copy-start(bf16[1,128,2048]{2,1,0:T(8,128)(2,1)} %param.6) | copy-start | bytes 1572868
  8.0 155.0 %all-gather.3.cloned.1.call-start = ((), (), s32[]{:S(2)}) async-start(), calls=%async_computation.9 | async-start | bytes 10485760 | tf_op jit(solution)/shard_map/all_gather | solution.py:81
  11.7 33.6 %copy-start.7 = (bf16[1,128,2048]{2,1,0:T(8,128)(2,1)S(1)}, bf16[1,128,2048]{2,1,0:T(8,128)(2,1)}, u32[]{:S(2)}) copy-start(bf16[1,128,2048]{2,1,0:T(8,128)(2,1)} %param.7) | copy-start | bytes 1572868
  24.2 17.4 %all-to-all-start = ((bf16[2,2,65536]{2,1,0:T(2,128)(2,1)}), bf16[2,2,65536]{2,1,0:T(2,128)(2,1)S(1)}, u32[]{:S(2)}, u32[]{:S(2)}) async-start(bf16[2,2,65536]{2,1,0:T(2,128)(2,1)} %reshape.80), calls=%async_computation | async-start | bytes 1048576 | tf_op jit(solution)/shard_map/all_to_all | solution.py:85
  41.6 16.9 %all-to-all-start.1 = ((bf16[2,2,65536]{2,1,0:T(2,128)(2,1)}), bf16[2,2,65536]{2,1,0:T(2,128)(2,1)S(1)}, u32[]{:S(2)}, u32[]{:S(2)}) async-start(bf16[2,2,65536]{2,1,0:T(2,128)(2,1)} %reshape.82), calls=%async_computation.1 | async-start | bytes 1048576 | tf_op jit(solution)/shard_map/all_to_all | solution.py:86
  58.5 12.2 %all-to-all-start.3 = ((bf16[2,2,65536]{2,1,0:T(2,128)(2,1)}), bf16[2,2,65536]{2,1,0:T(2,128)(2,1)S(1)}, u32[]{:S(2)}, u32[]{:S(2)}) async-start(bf16[2,2,65536]{2,1,0:T(2,128)(2,1)} %reshape.78), calls=%async_computation.3 | async-start | bytes 1048576 | tf_op jit(solution)/shard_map/all_to_all | solution.py:87
  62.0 370.5 %reduce-scatter.2.cloned.1.call-start = ((), (), s32[]{:S(2)}) async-start(), calls=%async_computation.10 | async-start | bytes 18874368 | tf_op jit(solution)/shard_map/reduce_scatter | solution.py:97
  71.5 11.1 %copy-start.13 = (bf16[1,2,128,1024]{3,2,1,0:T(8,128)(2,1)}, bf16[1,2,128,1024]{3,2,1,0:T(8,128)(2,1)S(1)}, u32[]{:S(2)}) copy-start(bf16[1,2,128,1024]{3,2,1,0:T(8,128)(2,1)S(1)} %copy.62) | copy-start | bytes 1572868
  81.0 1.6 copy-start.3
  82.9 0.8 copy-start.11
  172.5 34.8 %copy-start.4 = (f32[256,256]{0,1:T(8,128)S(1)}, f32[256,256]{0,1:T(8,128)}, u32[]{:S(2)}) copy-start(f32[256,256]{0,1:T(8,128)} %copy-done.3) | copy-start | bytes 786436
  207.3 1.9 copy-start.15
  208.9 16.1 %copy-start.2 = (bf16[1,2,128,1024]{3,2,1,0:T(8,128)(2,1)S(1)}, bf16[1,2,128,1024]{3,2,1,0:T(8,128)(2,1)}, u32[]{:S(2)}) copy-start(bf16[1,2,128,1024]{3,2,1,0:T(8,128)(2,1)} %copy.56) | copy-start | bytes 1572868
  209.1 0.8 copy-start.12
  216.9 8.3 %copy-start.5 = (bf16[1,2,128,1024]{3,2,1,0:T(8,128)(2,1)S(1)}, bf16[1,2,128,1024]{3,2,1,0:T(8,128)(2,1)}, u32[]{:S(2)}) copy-start(bf16[1,2,128,1024]{3,2,1,0:T(8,128)(2,1)} %copy.58) | copy-start | bytes 1572868
  219.1 260.7 %all-to-all-start.6 = ((bf16[2,2,65536]{2,1,0:T(2,128)(2,1)}), bf16[2,2,65536]{2,1,0:T(2,128)(2,1)S(1)}, u32[]{:S(2)}, u32[]{:S(2)}) async-start(bf16[2,2,65536]{2,1,0:T(2,128)(2,1)} %reshape.88), calls=%async_computation.6 | async-start | bytes 1048576 | tf_op jit(solution)/shard_map/all_to_all | solution.py:95
  222.6 248.7 %all-reduce.2.cloned.1.call-start = ((), (), s32[]{:S(2)}) async-start(), calls=%async_computation.11 | async-start | bytes 2097152 | tf_op jit(solution)/shard_map/psum | solution.py:103
  222.6 4.5 copy-start.14
  222.6 4.5 copy-start.16
  228.6 0.8 copy-start.8
  229.6 0.8 copy-start.10
  230.4 205.1 %copy-start.9 = (bf16[256,1024]{0,1:T(8,128)(2,1)S(1)}, bf16[256,1024]{0,1:T(8,128)(2,1)}, u32[]{:S(2)}) copy-start(bf16[256,1024]{0,1:T(8,128)(2,1)} %copy-done.8) | copy-start | bytes 1572868
  435.3 81.6 %all-gather.5.cloned.1.call-start = ((), (), s32[]{:S(2)}) async-start(), calls=%async_computation.12 | async-start | bytes 3145728 | tf_op jit(solution)/shard_map/all_gather | solution.py:104
  479.8 17.5 %all-to-all-start.4 = ((bf16[2,2,65536]{2,1,0:T(2,128)(2,1)}), bf16[2,2,65536]{2,1,0:T(2,128)(2,1)S(1)}, u32[]{:S(2)}, u32[]{:S(2)}) async-start(bf16[2,2,65536]{2,1,0:T(2,128)(2,1)} %reshape.84), calls=%async_computation.4 | async-start | bytes 1048576 | tf_op jit(solution)/shard_map/all_to_all | solution.py:93
  497.3 17.3 %all-to-all-start.5 = ((bf16[2,2,65536]{2,1,0:T(2,128)(2,1)}), bf16[2,2,65536]{2,1,0:T(2,128)(2,1)S(1)}, u32[]{:S(2)}, u32[]{:S(2)}) async-start(bf16[2,2,65536]{2,1,0:T(2,128)(2,1)} %reshape.86), calls=%async_computation.5 | async-start | bytes 1048576 | tf_op jit(solution)/shard_map/all_to_all | solution.py:94
  515.3 5.7 %copy-start.1 = (bf16[1,128,2048]{2,1,0:T(8,128)(2,1)S(1)}, bf16[1,128,2048]{2,1,0:T(8,128)(2,1)}, u32[]{:S(2)}) copy-start(bf16[1,128,2048]{2,1,0:T(8,128)(2,1)} %param.8) | copy-start | bytes 1572868
Sparse Core Ops, SparseCore 0:
  10.4 152.5 all-gather.2
Sparse Core Ops, SparseCore 1:
  115.1 317.4 reduce-scatter.1
  435.4 35.7 all-reduce.1
  472.7 44.1 all-gather.4
where the time goes:
time: 538 us; the launch traced here: 529 us
  waiting for transfers between devices  305 us (57%)
  other arithmetic  73.5 us (14%)
  local copies, waits for them, and re-layouts  44.6 us (8%)
  matrix products  38.3 us (7%)
  blocking collectives  28.8 us (5%)
  starting transfers between devices  22.2 us (4%)
  between operations  16.5 us (3%)
    reduce_scatter x1, waiting for transfers between devices, body(): lax.psum_scatter(jnp.einsum('btr,btd->rd', attended, cotangent, preferred...  201 us
    unnamed x8, other arithmetic  63.6 us
    all_gather x1, waiting for transfers between devices, body(): lax.all_gather(out_weight, 'fsdp', axis=0, tiled=True)  48.1 us
    psum x1, waiting for transfers between devices, body(): shares = lax.psum(shares.astype(jnp.bfloat16), 'dp').astype(jnp.float32)  34.4 us
    unnamed x65, local copies, waits for them, and re-layouts  28.2 us
    all_to_all x1, blocking collectives, body(): lax.all_to_all(grad_out, 'seq', split_axis=2, concat_axis=1, tiled=True)  17.7 us
    all_to_all x1, blocking collectives, body(): lax.all_to_all(head_results[0], 'seq', split_axis=1, concat_axis=2, tiled...  11.1 us
  transfers between devices with their start and end apart: 10, of which 7 were waited for; matrix products, arithmetic and copies ran while one was open for 28% of the time, Pallas kernels for 0%

commit v1 on v0

--- a/solution.py
+++ b/solution.py
@@ -4,6 +4,19 @@
 from jax.sharding import PartitionSpec as P
 
 DH = 128
+
+
+def collect(shard, axis, dim):
+    ways = lax.axis_size(axis)
+    up = [(d, (d + 1) % ways) for d in range(ways)]
+    down = [(d, (d - 1) % ways) for d in range(ways)]
+    earlier, later = ([shard], [shard])
+    for _ in range(ways // 2):
+        earlier.append(lax.ppermute(earlier[-1], axis, up))
+    for _ in range((ways - 1) // 2):
+        later.append(lax.ppermute(later[-1], axis, down))
+    line = jnp.concatenate([*earlier[::-1], *later[1:]], axis=dim)
+    return jnp.roll(line, (lax.axis_index(axis) - ways // 2) * shard.shape[dim], axis=dim)
 
 
 def head_backward(query_head, key_head, value_head, grad_head, block_rows):
@@ -76,10 +89,7 @@
 def body(queries, key_rows, value_rows, cotangent, out_weight):
     samples = lax.axis_size("dp") * lax.axis_size("fsdp")
     grad_out = jnp.einsum(
-        "btd,rd->btr",
-        cotangent,
-        lax.all_gather(out_weight, "fsdp", axis=0, tiled=True),
-        preferred_element_type=jnp.float32,
+        "btd,rd->btr", cotangent, collect(out_weight, "fsdp", 0), preferred_element_type=jnp.float32
     ).astype(jnp.bfloat16)
     query_heads, key_heads, value_heads, grad_heads = (
         lax.all_to_all(queries, "seq", split_axis=2, concat_axis=1, tiled=True),

time: 538 us -> 636 us (1.18)
  starting transfers between devices: 22.2 us -> 64.6 us
  matrix products: 38.3 us -> 62 us
  local copies, waits for them, and re-layouts: 44.6 us -> 67 us
  waiting for transfers between devices: 305 us -> 314 us
    ppermute x0 -> x3, waiting for transfers between devices: none -> 227 us  [the longest x2 158 us: collect(): earlier.append(lax.ppermute(earlier[-1], axis, up))]
    reduce_scatter x1, waiting for transfers between devices: 201 us -> 42 us  [body(): lax.psum_scatter(jnp.einsum('btr,btd->rd', attended, cotangent, preferred...]
    all_gather x1 -> x0, waiting for transfers between devices: 48.1 us -> none  [body(): lax.all_gather(out_weight, 'fsdp', axis=0, tiled=True)]
    ppermute x0 -> x3, starting transfers between devices: none -> 41.8 us  [the longest x1 22.8 us: collect(): later.append(lax.ppermute(later[-1], axis, down))]
    unnamed x65 -> x108, local copies, waits for them, and re-layouts: 28.2 us -> 41.1 us
    dot_general x8, matrix products: 3.64 us -> 13.1 us  [visit(): jnp.einsum('qk,qd->kd', grad_scores, query_block, preferred_element_type=...]
    dot_general x8, matrix products: 1.83 us -> 10.8 us  [visit(): jnp.einsum('qk,qd->kd', weights_half, grad_block, preferred_element_type=...]
    dot_general x8, matrix products: 1.74 us -> 8.82 us  [visit(): jnp.einsum('qk,kd->qd', grad_scores, key_head, preferred_element_type=jnp...]
  transfers between devices with their start and end apart: 10 -> 12, of which waited for: 7 -> 8; matrix products, arithmetic and copies ran while one was open for 28% -> 24% of each run, Pallas kernels for 0% -> 0%
where the time goes in v1:
time: 636 us; the launch traced here: 625 us
  waiting for transfers between devices  314 us (49%)
  other arithmetic  77.5 us (12%)
  local copies, waits for them, and re-layouts  67 us (11%)
  starting transfers between devices  64.6 us (10%)
  matrix products  62 us (10%)
  blocking collectives  25.4 us (4%)
  between operations  15.1 us (2%)
    ppermute x2, waiting for transfers between devices, collect(): earlier.append(lax.ppermute(earlier[-1], axis, up))  158 us
    ppermute x1, waiting for transfers between devices, collect(): later.append(lax.ppermute(later[-1], axis, down))  68.7 us
    unnamed x8, other arithmetic  63 us
    reduce_scatter x1, waiting for transfers between devices, body(): lax.psum_scatter(jnp.einsum('btr,btd->rd', attended, cotangent, preferred...  42 us
    unnamed x108, local copies, waits for them, and re-layouts  41.1 us
    psum x1, waiting for transfers between devices, body(): shares = lax.psum(shares.astype(jnp.bfloat16), 'dp').astype(jnp.float32)  31.3 us
    ppermute x1, starting transfers between devices, collect(): later.append(lax.ppermute(later[-1], axis, down))  22.8 us
    ppermute x2, starting transfers between devices, collect(): earlier.append(lax.ppermute(earlier[-1], axis, up))  19 us
  transfers between devices with their start and end apart: 12, of which 8 were waited for; matrix products, arithmetic and copies ran while one was open for 24% of the time, Pallas kernels for 0%

profile of v1, /device:TPU:0, one launch (start us, length us, event | category | flops | bytes accessed | tf_op | source)
XLA Modules:
  0.0 625.4 jit_solution(1327228646953020909)
XLA Ops:
  7.2 2.4 copy.57
  10.1 11.5 %reduce = bf16[2048,128]{1,0:T(8,128)(2,1)S(1)} reduce(bf16[2048,1,128]{2,1,0:T(2,128)(2,1)S(1)} %bitcast.296, bf16[]{:T(256)} %broadcast.91), dimensions={1}, to_apply=%bitcast.179.reduce_sub_computation | reduce | bytes 1048578
  22.5 4.2 all-to-all-start.1
  26.7 2.3 copy.55
  29.1 11.5 %reduce.1 = bf16[2048,128]{1,0:T(8,128)(2,1)S(1)} reduce(bf16[2048,1,128]{2,1,0:T(2,128)(2,1)S(1)} %bitcast.302, bf16[]{:T(256)} %broadcast.91), dimensions={1}, to_apply=%bitcast.177.reduce_sub_computation | reduce | bytes 1048578
  41.4 3.7 all-to-all-start
  45.2 2.4 copy.61
  47.6 11.5 %reduce.2 = bf16[2048,128]{1,0:T(8,128)(2,1)S(1)} reduce(bf16[2048,1,128]{2,1,0:T(2,128)(2,1)S(1)} %bitcast.303, bf16[]{:T(256)} %broadcast.91), dimensions={1}, to_apply=%bitcast.175.reduce_sub_computation | reduce | bytes 1048578
  60.7 4.2 all-to-all-start.3
  69.7 4.1 all-to-all-done.3
  73.8 1.4 reshape.79
  76.1 1.2 copy.62
  86.4 2.5 copy.69
  88.9 4.5 reduce.7
  93.4 1.4 reshape.90
  94.8 10.8 %all_to_all.141 = bf16[2,2,65536]{2,1,0:T(2,128)(2,1)} all-to-all(bf16[2,2,65536]{2,1,0:T(2,128)(2,1)S(1)} %reshape.90), channel_id=1, replica_groups=mesh['dp'=4,'fsdp'=4,'seq'=2] {'seq'}, dimensions={0} | all-to-all | bytes 1048576 | tf_op jit(solution)/shard_map/all_to_all | solution.py:102
  105.6 1.4 reshape.91
  108.0 2.0 copy.70
  110.1 9.2 %fusion.56 = f32[2048,2048]{1,0:T(8,128)} fusion(bf16[128,2048]{0,1:T(8,128)(2,1)} %bitcast.304, bf16[1,128,2048]{2,1,0:T(8,128)(2,1)S(1)} %copy-done), kind=kOutput, calls=%fused_computation.93 | convolution fusion | flops 1073741824 | bytes 17825792 | tf_op jit(solution)/shard_map/btr,btd->rd/dot_general | solution.py:108
  119.3 1.6 collective-permute-start
  120.9 85.3 %collective-permute-done = bf16[512,2048]{1,0:T(8,128)(2,1)} collective-permute-done((bf16[512,2048]{1,0:T(8,128)(2,1)S(1)}, bf16[512,2048]{1,0:T(8,128)(2,1)}, u32[]{:S(2)}, u32[]{:S(2)}) %collective-permute-start) | collective-permute-done | bytes 2097184 | tf_op jit(solution)/shard_map/ppermute | solution.py:15
  206.2 17.5 %collective-permute-start.1 = (bf16[512,2048]{1,0:T(8,128)(2,1)}, bf16[512,2048]{1,0:T(8,128)(2,1)}, u32[]{:S(2)}, u32[]{:S(2)}) collective-permute-start(bf16[512,2048]{1,0:T(8,128)(2,1)} %collective-permute-done), channel_id=1, source_target_pairs={{0,2},{2,4},{4,6},{6,0},{1,3},{3,5},{5,7},{7,1},{8,10},{10,12},{12... | collective-permute-start | bytes 6291464 | tf_op jit(solution)/shard_map/ppermute | solution.py:15
  223.7 22.8 %collective-permute-start.2 = (bf16[512,2048]{1,0:T(8,128)(2,1)S(1)}, bf16[512,2048]{1,0:T(8,128)(2,1)}, u32[]{:S(2)}, u32[]{:S(2)}) collective-permute-start(bf16[512,2048]{1,0:T(8,128)(2,1)S(1)} %copy-done.1), channel_id=1, source_target_pairs={{0,6},{2,0},{4,2},{6,4},{1,7},{3,1},{5,3},{7,5},{8,14},{10,8},{12,... | collective-permute-start | bytes 6291464 | tf_op jit(solution)/shard_map/ppermute | solution.py:17
  246.5 73.0 %collective-permute-done.1 = bf16[512,2048]{1,0:T(8,128)(2,1)} collective-permute-done((bf16[512,2048]{1,0:T(8,128)(2,1)}, bf16[512,2048]{1,0:T(8,128)(2,1)}, u32[]{:S(2)}, u32[]{:S(2)}) %collective-permute-start.1) | collective-permute-done | bytes 2097184 | tf_op jit(solution)/shard_map/ppermute | solution.py:15
  319.4 1.7 constant_dynamic-update-slice_fusion.7
  321.2 1.8 constant_dynamic-update-slice_fusion.6
  323.2 68.7 %collective-permute-done.2 = bf16[512,2048]{1,0:T(8,128)(2,1)} collective-permute-done((bf16[512,2048]{1,0:T(8,128)(2,1)S(1)}, bf16[512,2048]{1,0:T(8,128)(2,1)}, u32[]{:S(2)}, u32[]{:S(2)}) %collective-permute-start.2) | collective-permute-done | bytes 2097184 | tf_op jit(solution)/shard_map/ppermute | solution.py:17
  391.9 1.7 constant_dynamic-update-slice_fusion.4
  393.6 1.7 constant_dynamic-update-slice_fusion.3
  395.4 1.8 constant_dynamic-update-slice_fusion.2
  397.4 1.9 constant_dynamic-update-slice_fusion
  399.3 2.4 fusion.5
  401.8 8.1 %copy.83 = bf16[1,128,2048]{1,0,2:T(2,128)(2,1)S(1)} copy(bf16[1,128,2048]{1,2,0:T(8,128)(2,1)S(1)} %fusion.5) | data formatting | bytes 1048576 | tf_op jit(solution)/shard_map/convert_element_type | solution.py:93
  409.9 12.3 %reduce.3 = bf16[2048,128]{1,0:T(8,128)(2,1)} reduce(bf16[2048,1,128]{2,1,0:T(2,128)(2,1)S(1)} %bitcast.299, bf16[]{:T(256)} %broadcast.91), dimensions={1}, to_apply=%bitcast.271.reduce_sub_computation | reduce | bytes 1048578
  423.3 14.6 %all_to_all.142 = bf16[2,2,65536]{2,1,0:T(2,128)(2,1)} all-to-all(bf16[2,2,65536]{2,1,0:T(2,128)(2,1)S(1)} %reshape.76), channel_id=1, replica_groups=mesh['dp'=4,'fsdp'=4,'seq'=2] {'seq'}, dimensions={0} | all-to-all | bytes 1048576 | tf_op jit(solution)/shard_map/all_to_all | solution.py:98
  437.9 1.4 reshape.77
  440.2 1.2 copy.60
  441.4 1.4 multiply_reduce_fusion.7
  464.6 2.5 copy.63
  467.1 4.5 reduce.4
  471.6 2.1 reshape.84
  473.6 3.5 all-to-all-start.4
  477.2 1.8 fusion.25
  478.9 1.8 fusion.27
  480.7 1.8 fusion.29
  482.5 1.8 fusion.31
  484.2 1.8 fusion.33
  486.0 42.0 %reduce-scatter.2.cloned.1.call-done = f32[256,2048]{1,0:T(8,128)} async-done(((f32[2048,2048]{1,0:T(8,128)}), f32[256,2048]{1,0:T(8,128)}) %reduce-scatter.2.cloned.1.call-update) | async-done | bytes 2097168 | tf_op jit(solution)/shard_map/reduce_scatter | solution.py:107
  528.0 2.7 convert_element_type.244
  530.8 1.8 fusion.35
  534.9 31.3 %all-reduce.2.cloned.1.call-done = bf16[256,2048]{1,0:T(8,128)(2,1)} async-done(((bf16[256,2048]{1,0:T(8,128)(2,1)}), bf16[256,2048]{1,0:T(8,128)(2,1)}) %all-reduce.2.cloned.1.call-update) | async-done | bytes 1048592 | tf_op jit(solution)/shard_map/psum | solution.py:113
  566.2 1.8 fusion.37
  572.2 2.7 copy.65
  574.9 3.7 reduce.5
  579.7 1.7 fusion.50
  581.4 3.5 all-to-all-start.5
  584.9 1.7 fusion.49
  586.6 1.7 fusion.48
  588.3 2.5 copy.67
  590.8 3.7 reduce.6
  595.6 3.8 all-to-all-done.5
  599.4 3.5 all-to-all-start.6
  606.8 5.4 all-to-all-done.6
  614.2 4.2 convert_multiply_fusion
  (163 shorter events, 58.0 us)
Async XLA Ops:
  7.2 102.9 %copy-start = (bf16[1,128,2048]{2,1,0:T(8,128)(2,1)S(1)}, bf16[1,128,2048]{2,1,0:T(8,128)(2,1)}, u32[]{:S(2)}) copy-start(bf16[1,128,2048]{2,1,0:T(8,128)(2,1)} %param.8) | copy-start | bytes 1572868
  22.5 18.9 %all-to-all-start.1 = ((bf16[2,2,65536]{2,1,0:T(2,128)(2,1)}), bf16[2,2,65536]{2,1,0:T(2,128)(2,1)S(1)}, u32[]{:S(2)}, u32[]{:S(2)}) async-start(bf16[2,2,65536]{2,1,0:T(2,128)(2,1)} %reshape.82), calls=%async_computation.1 | async-start | bytes 1048576 | tf_op jit(solution)/shard_map/all_to_all | solution.py:96
  41.4 19.3 %all-to-all-start = ((bf16[2,2,65536]{2,1,0:T(2,128)(2,1)}), bf16[2,2,65536]{2,1,0:T(2,128)(2,1)S(1)}, u32[]{:S(2)}, u32[]{:S(2)}) async-start(bf16[2,2,65536]{2,1,0:T(2,128)(2,1)} %reshape.80), calls=%async_computation | async-start | bytes 1048576 | tf_op jit(solution)/shard_map/all_to_all | solution.py:95
  60.7 9.0 %copy-start.10 = (bf16[1,2,128,1024]{3,2,1,0:T(8,128)(2,1)}, bf16[1,2,128,1024]{3,2,1,0:T(8,128)(2,1)S(1)}, u32[]{:S(2)}) copy-start(bf16[1,2,128,1024]{3,2,1,0:T(8,128)(2,1)S(1)} %copy.58) | copy-start | bytes 1572868
  60.7 13.1 %all-to-all-start.3 = ((bf16[2,2,65536]{2,1,0:T(2,128)(2,1)}), bf16[2,2,65536]{2,1,0:T(2,128)(2,1)}, u32[]{:S(2)}, u32[]{:S(2)}) async-start(bf16[2,2,65536]{2,1,0:T(2,128)(2,1)} %reshape.78), calls=%async_computation.3 | async-start | bytes 1048576 | tf_op jit(solution)/shard_map/all_to_all | solution.py:97
  65.0 463.0 %reduce-scatter.2.cloned.1.call-start = ((), (), s32[]{:S(2)}) async-start(), calls=%async_computation.9 | async-start | bytes 18874368 | tf_op jit(solution)/shard_map/reduce_scatter | solution.py:107
  66.7 376.1 %copy-start.26 = (f32[256]{0:T(256)}, f32[256]{0:T(256)S(1)}, u32[]{:S(2)}) copy-start(f32[256]{0:T(256)S(1)} %get-tuple-element.152) | copy-start | bytes 3076
  67.6 378.6 %copy-start.25 = (f32[256]{0:T(256)}, f32[256]{0:T(256)S(1)}, u32[]{:S(2)}) copy-start(f32[256]{0:T(256)S(1)} %get-tuple-element.165) | copy-start | bytes 3076
  68.5 381.1 %copy-start.24 = (f32[256]{0:T(256)}, f32[256]{0:T(256)S(1)}, u32[]{:S(2)}) copy-start(f32[256]{0:T(256)S(1)} %get-tuple-element.169) | copy-start | bytes 3076
  68.8 41.3 %copy-start.8 = (f32[256,256]{0,1:T(8,128)}, f32[256,256]{0,1:T(8,128)S(1)}, u32[]{:S(2)}) copy-start(f32[256,256]{0,1:T(8,128)S(1)} %get-tuple-element.183) | copy-start | bytes 786436
  68.8 384.1 %copy-start.23 = (f32[256]{0:T(256)}, f32[256]{0:T(256)S(1)}, u32[]{:S(2)}) copy-start(f32[256]{0:T(256)S(1)} %get-tuple-element.182) | copy-start | bytes 3076
  69.0 41.0 %copy-start.6 = (f32[256,256]{0,1:T(8,128)}, f32[256,256]{0,1:T(8,128)S(1)}, u32[]{:S(2)}) copy-start(f32[256,256]{0,1:T(8,128)S(1)} %get-tuple-element.187) | copy-start | bytes 786436
  69.2 40.8 %copy-start.4 = (f32[256,256]{0,1:T(8,128)}, f32[256,256]{0,1:T(8,128)S(1)}, u32[]{:S(2)}) copy-start(f32[256,256]{0,1:T(8,128)S(1)} %get-tuple-element.200) | copy-start | bytes 786436
  69.5 40.6 %copy-start.2 = (f32[256,256]{0,1:T(8,128)}, f32[256,256]{0,1:T(8,128)S(1)}, u32[]{:S(2)}) copy-start(f32[256,256]{0,1:T(8,128)S(1)} %get-tuple-element.204) | copy-start | bytes 786436
  77.4 8.3 %copy-start.20 = (bf16[1,2,128,1024]{3,2,1,0:T(8,128)(2,1)}, bf16[1,2,128,1024]{3,2,1,0:T(8,128)(2,1)S(1)}, u32[]{:S(2)}) copy-start(bf16[1,2,128,1024]{3,2,1,0:T(8,128)(2,1)S(1)} %copy.62) | copy-start | bytes 1572868
  78.6 364.3 %copy-start.34 = (f32[256]{0:T(256)}, f32[256]{0:T(256)S(1)}, u32[]{:S(2)}) copy-start(f32[256]{0:T(256)S(1)} %fusion.60) | copy-start | bytes 3076
  79.6 366.6 %copy-start.33 = (f32[256]{0:T(256)}, f32[256]{0:T(256)S(1)}, u32[]{:S(2)}) copy-start(f32[256]{0:T(256)S(1)} %fusion.62) | copy-start | bytes 3076
  80.6 369.0 %copy-start.32 = (f32[256]{0:T(256)}, f32[256]{0:T(256)S(1)}, u32[]{:S(2)}) copy-start(f32[256]{0:T(256)S(1)} %fusion.64) | copy-start | bytes 3076
  80.7 372.2 %copy-start.31 = (f32[256]{0:T(256)}, f32[256]{0:T(256)S(1)}, u32[]{:S(2)}) copy-start(f32[256]{0:T(256)S(1)} %fusion.66) | copy-start | bytes 3076
  80.8 374.4 %copy-start.30 = (f32[256]{0:T(256)}, f32[256]{0:T(256)S(1)}, u32[]{:S(2)}) copy-start(f32[256]{0:T(256)S(1)} %fusion.68) | copy-start | bytes 3076
  80.9 376.6 %copy-start.29 = (f32[256]{0:T(256)}, f32[256]{0:T(256)S(1)}, u32[]{:S(2)}) copy-start(f32[256]{0:T(256)S(1)} %fusion.70) | copy-start | bytes 3076
  80.9 378.8 %copy-start.28 = (f32[256]{0:T(256)}, f32[256]{0:T(256)S(1)}, u32[]{:S(2)}) copy-start(f32[256]{0:T(256)S(1)} %fusion.72) | copy-start | bytes 3076
  81.0 380.0 %copy-start.27 = (f32[256]{0:T(256)}, f32[256]{0:T(256)S(1)}, u32[]{:S(2)}) copy-start(f32[256]{0:T(256)S(1)} %fusion.74) | copy-start | bytes 3076
  85.6 0.8 copy-start.13
  110.1 9.3 %copy-start.1 = (bf16[512,2048]{1,0:T(8,128)(2,1)S(1)}, bf16[512,2048]{1,0:T(8,128)(2,1)}, u32[]{:S(2)}) copy-start(bf16[512,2048]{1,0:T(8,128)(2,1)} %param.9) | copy-start | bytes 6291460
  119.3 86.9 %collective-permute-start = (bf16[512,2048]{1,0:T(8,128)(2,1)S(1)}, bf16[512,2048]{1,0:T(8,128)(2,1)}, u32[]{:S(2)}, u32[]{:S(2)}) collective-permute-start(bf16[512,2048]{1,0:T(8,128)(2,1)S(1)} %copy-done.1), channel_id=1, source_target_pairs={{0,2},{2,4},{4,6},{6,0},{1,3},{3,5},{5,7},{7,1},{8,10},{10,12},{12... | collective-permute-start | bytes 6291464 | tf_op jit(solution)/shard_map/ppermute | solution.py:15
  206.2 113.2 %collective-permute-start.1 = (bf16[512,2048]{1,0:T(8,128)(2,1)}, bf16[512,2048]{1,0:T(8,128)(2,1)}, u32[]{:S(2)}, u32[]{:S(2)}) collective-permute-start(bf16[512,2048]{1,0:T(8,128)(2,1)} %collective-permute-done), channel_id=1, source_target_pairs={{0,2},{2,4},{4,6},{6,0},{1,3},{3,5},{5,7},{7,1},{8,10},{10,12},{12... | collective-permute-start | bytes 6291464 | tf_op jit(solution)/shard_map/ppermute | solution.py:15
  223.7 168.2 %collective-permute-start.2 = (bf16[512,2048]{1,0:T(8,128)(2,1)S(1)}, bf16[512,2048]{1,0:T(8,128)(2,1)}, u32[]{:S(2)}, u32[]{:S(2)}) collective-permute-start(bf16[512,2048]{1,0:T(8,128)(2,1)S(1)} %copy-done.1), channel_id=1, source_target_pairs={{0,6},{2,0},{4,2},{6,4},{1,7},{3,1},{5,3},{7,5},{8,14},{10,8},{12,... | collective-permute-start | bytes 6291464 | tf_op jit(solution)/shard_map/ppermute | solution.py:17
  397.4 54.4 %copy-start.9 = (f32[256,256]{0,1:T(8,128)S(1)}, f32[256,256]{0,1:T(8,128)}, u32[]{:S(2)}) copy-start(f32[256,256]{0,1:T(8,128)} %copy-done.8) | copy-start | bytes 786436
  397.4 56.7 %copy-start.7 = (f32[256,256]{0,1:T(8,128)S(1)}, f32[256,256]{0,1:T(8,128)}, u32[]{:S(2)}) copy-start(f32[256,256]{0,1:T(8,128)} %copy-done.6) | copy-start | bytes 786436
  399.3 57.1 %copy-start.5 = (f32[256,256]{0,1:T(8,128)S(1)}, f32[256,256]{0,1:T(8,128)}, u32[]{:S(2)}) copy-start(f32[256,256]{0,1:T(8,128)} %copy-done.4) | copy-start | bytes 786436
  399.3 59.4 %copy-start.3 = (f32[256,256]{0,1:T(8,128)S(1)}, f32[256,256]{0,1:T(8,128)}, u32[]{:S(2)}) copy-start(f32[256,256]{0,1:T(8,128)} %copy-done.2) | copy-start | bytes 786436
  441.4 22.3 %copy-start.21 = (bf16[1,2,128,1024]{3,2,1,0:T(8,128)(2,1)}, bf16[1,2,128,1024]{3,2,1,0:T(8,128)(2,1)S(1)}, u32[]{:S(2)}) copy-start(bf16[1,2,128,1024]{3,2,1,0:T(8,128)(2,1)S(1)} %copy.60) | copy-start | bytes 1572868
  443.9 2.3 copy-start.22
  447.3 12.5 %copy-start.15 = (bf16[256,256]{0,1:T(8,128)(2,1)}, bf16[256,256]{0,1:T(8,128)(2,1)S(1)}, u32[]{:S(2)}) copy-start(bf16[256,256]{0,1:T(8,128)(2,1)S(1)} %multiply_convert_fusion.6) | copy-start | bytes 393220
  450.7 13.1 %copy-start.16 = (bf16[256,256]{0,1:T(8,128)(2,1)}, bf16[256,256]{0,1:T(8,128)(2,1)S(1)}, u32[]{:S(2)}) copy-start(bf16[256,256]{0,1:T(8,128)(2,1)S(1)} %multiply_convert_fusion.5) | copy-start | bytes 393220
  453.0 4.5 copy-start.18
  455.2 8.6 %copy-start.19 = (bf16[256,256]{0,1:T(8,128)(2,1)}, bf16[256,256]{0,1:T(8,128)(2,1)S(1)}, u32[]{:S(2)}) copy-start(bf16[256,256]{0,1:T(8,128)(2,1)S(1)} %multiply_convert_fusion.3) | copy-start | bytes 393220
  457.6 6.2 copy-start.17
  459.9 4.0 copy-start.14
  463.8 0.8 copy-start.11
  473.6 107.8 %all-to-all-start.4 = ((bf16[2,2,65536]{2,1,0:T(2,128)(2,1)}), bf16[2,2,65536]{2,1,0:T(2,128)(2,1)S(1)}, u32[]{:S(2)}, u32[]{:S(2)}) async-start(bf16[2,2,65536]{2,1,0:T(2,128)(2,1)} %reshape.84), calls=%async_computation.4 | async-start | bytes 1048576 | tf_op jit(solution)/shard_map/all_to_all | solution.py:103
  477.1 89.1 %all-reduce.2.cloned.1.call-start = ((), (), s32[]{:S(2)}) async-start(), calls=%async_computation.10 | async-start | bytes 2097152 | tf_op jit(solution)/shard_map/psum | solution.py:113
  530.7 83.5 %all-gather.2.cloned.1.call-start = ((), (), s32[]{:S(2)}) async-start(), calls=%async_computation.11 | async-start | bytes 3145728 | tf_op jit(solution)/shard_map/all_gather | solution.py:114
  571.3 0.9 copy-start.12
  581.4 18.0 %all-to-all-start.5 = ((bf16[2,2,65536]{2,1,0:T(2,128)(2,1)}), bf16[2,2,65536]{2,1,0:T(2,128)(2,1)S(1)}, u32[]{:S(2)}, u32[]{:S(2)}) async-start(bf16[2,2,65536]{2,1,0:T(2,128)(2,1)} %reshape.86), calls=%async_computation.5 | async-start | bytes 1048576 | tf_op jit(solution)/shard_map/all_to_all | solution.py:104
  599.4 12.9 %all-to-all-start.6 = ((bf16[2,2,65536]{2,1,0:T(2,128)(2,1)}), bf16[2,2,65536]{2,1,0:T(2,128)(2,1)S(1)}, u32[]{:S(2)}, u32[]{:S(2)}) async-start(bf16[2,2,65536]{2,1,0:T(2,128)(2,1)} %reshape.88), calls=%async_computation.6 | async-start | bytes 1048576 | tf_op jit(solution)/shard_map/all_to_all | solution.py:105
Sparse Core Ops, SparseCore 0:
  119.4 408.4 reduce-scatter.1
  531.0 35.1 all-reduce.1
  567.8 40.7 all-gather.1
